TPU v7x, 128 devices: a whole 4x4x4 slice. The times are simulated.
128 devices in a mesh: dp: 32 (over x, y, core), ctx: 4 (over z).
Axes of the slice: x: 4, y: 4, z: 4, core: 2. Of those that a mesh axis runs over, the one named last changes fastest.
Arguments:
- tokens: bfloat16 [65536, 576], P(('dp', 'ctx')), may hold values from -6 to 6
- cotangent: bfloat16 [65536, 576], P(('dp', 'ctx')), may hold values from -6 to 6
- w_qkv: float32 [576, 960], P('ctx'), may hold values from -0.375 to 0.375
- w_out: float32 [576, 576], P('ctx'), may hold values from -0.75 to 0.75
- w_gate_up: float32 [576, 3072], P('ctx'), may hold values from -0.25 to 0.25
- w_down: float32 [1536, 576], P('ctx'), may hold values from -0.15625 to 0.15625
- vectors: float32 [2112], P('ctx'), may hold values from -1 to 1.4, as said below
- first_qkv: float32 [576, 960], P('ctx'), may hold values from -128 to 128
- first_out: float32 [576, 576], P('ctx'), may hold values from -64 to 64
- first_gate_up: float32 [576, 3072], P('ctx'), may hold values from -48 to 48
- first_down: float32 [1536, 576], P('ctx'), may hold values from -96 to 96
- first_vectors: float32 [2112], P('ctx'), may hold values from -160 to 160
- second_qkv: float32 [576, 960], P('ctx'), may hold values from 41.94304 to 167.77216
- second_out: float32 [576, 576], P('ctx'), may hold values from 8.51968 to 34.07872
- second_gate_up: float32 [576, 3072], P('ctx'), may hold values from 5.89824 to 23.59296
- second_down: float32 [1536, 576], P('ctx'), may hold values from 23.59296 to 94.37184
- second_vectors: float32 [2112], P('ctx'), may hold values from 65.536 to 262.144
Outputs:
- block_out: float32 [65536, 576], P(('dp', 'ctx'))
- input_grad: float32 [65536, 576], P(('dp', 'ctx'))
- new_qkv: float32 [576, 960], P('ctx')
- new_out: float32 [576, 576], P('ctx')
- new_gate_up: float32 [576, 3072], P('ctx')
- new_down: float32 [1536, 576], P('ctx')
- new_vectors: float32 [2112], P('ctx')
- moment_qkv: float32 [576, 960], P('ctx')
- moment_out: float32 [576, 576], P('ctx')
- moment_gate_up: float32 [576, 3072], P('ctx')
- moment_down: float32 [1536, 576], P('ctx')
- moment_vectors: float32 [2112], P('ctx')
- square_qkv: float32 [576, 960], P('ctx')
- square_out: float32 [576, 576], P('ctx')
- square_gate_up: float32 [576, 3072], P('ctx')
- square_down: float32 [1536, 576], P('ctx')
- square_vectors: float32 [2112], P('ctx')
Inputs may be any that keep to these rules, and one draw needn't show every extreme that they name: `vectors`: the first 1152 entries are the two norms' gains, the others the query, key and value biases.
All inputs are finite; a program needn't handle non-finite values.
Results may differ from a plain program's by a relative error of at most 0.013.
The roundings to bfloat16 on the way count: a program that leaves them out, or rounds other values in their place, can miss the bound.
Values may be sent and summed in bfloat16 or wider, within the bound.
A program may use at most 256 MiB of HBM per device.

v0:
```python
import functools

import jax
import jax.numpy as jnp
import numpy as np
from jax import lax
from jax.experimental import pallas as pl
from jax.experimental.pallas import tpu as pltpu
from jax.sharding import PartitionSpec as P

D = 576
HEADS = 9
KV_HEADS = 3
GROUP = 3
HEAD_DIM = 64
FF = 1536
STEP = 10
LEN = 2048
ROWS = 512
QW = 1024
OW = 640
VW = 2304
NX = 4
NY = 4
NZ = 4

EPS = 1e-05
ROPE_BASE = 100000.0
MASK_FILL = -1e30
BETA_ONE = 0.9
BETA_TWO = 0.999
ADAM_EPS = 1e-08
RATE_MATRIX = 0.05
RATE_VECTOR = 0.5
DECAY_MATRIX = 0.1

F32 = jnp.float32
BF16 = jnp.bfloat16
MESH = pl.DeviceIdType.MESH
VM = pltpu.VMEM
ANY = pl.ANY


def rope_tables():
    half = HEAD_DIM // 2
    exponent = np.arange(half, dtype=np.float32) * np.float32(2.0 / HEAD_DIM)
    inverse = (np.float64(ROPE_BASE) ** (-exponent.astype(np.float64))).astype(np.float32)
    angles = np.arange(LEN, dtype=np.float32)[:, None] * inverse[None, :]
    cosine = np.cos(angles.astype(np.float64)).astype(np.float32)
    sine = np.sin(angles.astype(np.float64)).astype(np.float32)
    cos_all = np.concatenate([cosine] * 4, axis=1)
    sin_all = np.concatenate([-sine, sine, -sine, sine], axis=1)
    return cos_all, sin_all


def dot(a, b, ca=1, cb=0):
    return lax.dot_general(a, b, (((ca,), (cb,)), ((), ())), preferred_element_type=F32)


def place():
    dp = lax.axis_index("dp")
    z = lax.axis_index("ctx")
    x = lax.div(dp, NY * 2)
    y = lax.rem(lax.div(dp, 2), NY)
    c = lax.rem(dp, 2)
    return x, y, c, z


def device(x, y, c, z):
    return (x * (NY * 2) + y * 2 + c, z)


def wrap(i, n):
    return lax.rem(i, n)


def remote(src, dst, ssem, rsem, dev):
    return pltpu.make_async_remote_copy(
        src_ref=src, dst_ref=dst, send_sem=ssem, recv_sem=rsem, device_id=dev, device_id_type=MESH
    )


def greet(peers):
    barrier = pltpu.get_barrier_semaphore()
    for peer in peers:
        pl.semaphore_signal(barrier, inc=1, device_id=peer, device_id_type=MESH)
    pl.semaphore_wait(barrier, len(peers))


def swap_halves(v):
    width = v.shape[1]
    lane = lax.broadcasted_iota(jnp.int32, v.shape, 1)
    down = pltpu.roll(v, width - 32, 1)
    up = pltpu.roll(v, 32, 1)
    return jnp.where(lax.rem(lane, 64) < 32, down, up)


def low_lanes(v):
    lane = lax.broadcasted_iota(jnp.int32, v.shape, 1)
    return lane < 64


class Reduction:
    @staticmethod
    def scratch(lead, r, w):
        dma = pltpu.SemaphoreType.DMA
        return [
            VM(lead + (r, w), BF16), VM((3, 4, r, w), BF16), VM((4, r, w), BF16),
            VM((3, r, w), BF16), VM((4, r, w), BF16), dma((6,)), dma((10,)),
        ]

    def __init__(self, own, fin, fin_at, bufs, swap, z_first):
        self.own, self.fin, self.fin_at, self.z_first = own, fin, fin_at, z_first
        self.rc, self.r1, self.s1, self.r2, self.r3, self.ss, self.rs = bufs
        x, y, c, z = place()
        self.c, self.z = c, z
        flip = c != swap
        self.a, self.b = jnp.where(flip, y, x), jnp.where(flip, x, y)
        self.at = lambda a, b, cc, zz: device(jnp.where(flip, b, a), jnp.where(flip, a, b), cc, zz)
        self.other = self.at(self.a, self.b, 1 - c, z)

    def copy(self, src, dst, k, dev, into=None):
        return remote(src, dst, self.ss.at[k], self.rs.at[k if into is None else into], dev)

    def whole(self, ref, k):
        return self.copy(ref, ref, k, self.other)

    def mine(self, a, z):
        return (self.c, z, a) if self.z_first else (self.c, a, z)

    def all_z(self, a):
        return self.own.at[self.c, :, a] if self.z_first else self.own.at[self.c, a]

    def core_copy(self, k):
        return self.copy(self.own.at[1 - self.c, k], self.rc.at[k], 0, self.other, 6 + k)

    def core_add(self, k):
        self.core_copy(k).wait_recv()

        def add(j, carry):
            self.own[self.c, k, j] = self.own[self.c, k, j] + self.rc[k, j]
            return carry

        lax.fori_loop(0, 4, add, 0)

    def core_all(self, act):
        def one(k, carry):
            act(k)
            return carry

        lax.fori_loop(0, 4, one, 0)

    def first_copy(self, d):
        to = wrap(self.a + d, 4)
        return self.copy(self.all_z(to), self.r1.at[d - 1], 1, self.at(to, self.b, self.c, self.z))

    def first_start(self):
        for d in range(1, 4):
            self.first_copy(d).start()

    def first_piece(self, piece):
        d = wrap(piece + 4 - self.a, 4)

        @pl.when(d > 0)
        def _():
            self.first_copy(jnp.maximum(d, 1)).start()

    def first_sum(self):
        self.whole(self.r1, 1).wait_recv()

        def add(j, carry):
            total = self.own[self.mine(self.a, j)].astype(F32) + self.r1[0, j].astype(F32)
            total = total + self.r1[1, j].astype(F32) + self.r1[2, j].astype(F32)
            self.s1[j] = total.astype(BF16)
            return carry

        lax.fori_loop(0, 4, add, 0)

    def z_start(self):
        for d in range(1, 4):
            to = wrap(self.z + d, 4)
            self.copy(self.s1.at[to], self.r2.at[d - 1], 2, self.at(self.a, self.b, self.c, to)).start()

    def z_sum(self):
        self.whole(self.r2, 2).wait_recv()
        total = self.s1[self.z].astype(F32) + self.r2[0].astype(F32)
        total = total + self.r2[1].astype(F32) + self.r2[2].astype(F32)
        self.r3[self.b] = total.astype(BF16)

    def exchange_start(self):
        for d in range(1, 4):
            to = wrap(self.b + d, 4)
            ref = self.r3.at[self.b]
            self.copy(ref, ref, 3, self.at(self.a, to, self.c, self.z)).start()

    def gather_start(self):
        self.whole(self.r3.at[0:3], 3).wait_recv()
        total = self.r3[0].astype(F32) + self.r3[1].astype(F32)
        total = total + self.r3[2].astype(F32) + self.r3[3].astype(F32)
        where = self.fin_at(self.c, self.a, 1)
        self.fin[where] = total.astype(BF16)
        ref = self.fin.at[where]
        for d in range(1, 4):
            self.copy(ref, ref, 4, self.at(wrap(self.a + d, 4), self.b, self.c, self.z)).start()

    def gather_forward(self):
        self.whole(self.fin.at[self.fin_at(0, 0, 3)], 4).wait_recv()
        ref = self.fin.at[self.fin_at(self.c, 0, 4)]
        self.copy(ref, ref, 5, self.other).start()

    def gather_wait(self):
        self.whole(self.fin.at[self.fin_at(0, 0, 4)], 5).wait_recv()

    def finish(self):
        for ref, k in (
            (self.rc, 0), (self.r1, 1), (self.r2, 2), (self.r3.at[0:3], 3),
            (self.fin.at[self.fin_at(0, 0, 3)], 4), (self.fin.at[self.fin_at(0, 0, 4)], 5),
        ):
            self.whole(ref, k).wait_send()


class VectorSum:
    SCRATCH = 4

    @staticmethod
    def scratch():
        dma = pltpu.SemaphoreType.DMA
        return [VM((2, 24, 128), F32), VM((3, 4, 24, 128), F32), dma((4,)), dma((4,))]

    def __init__(self, bufs):
        self.rc, self.r, self.ss, self.rs = bufs
        x, y, c, z = place()
        self.sibling = device(x, y, 1 - c, z)

    def copy(self, src, dst, k, dev):
        return remote(src, dst, self.ss.at[k], self.rs.at[k], dev)

    def stage(self, k):
        ref = self.rc.at[1] if k == 0 else self.r.at[k - 1, 0:3]
        return self.copy(ref, ref, k, self.sibling)

    def start(self):
        self.copy(self.rc.at[0], self.rc.at[1], 0, self.sibling).start()

    def next(self, k):
        x, y, c, z = place()
        self.stage(k).wait_recv()
        if k == 0:
            total = self.rc[0] + self.rc[1]
        else:
            total = self.r[k - 1, 0] + self.r[k - 1, 1] + self.r[k - 1, 2] + self.r[k - 1, 3]
        if k == 3:
            return total
        me = (y, z, x)[k]
        self.r[k, me] = total
        for d in range(1, 4):
            to = wrap(me + d, 4)
            dev = (device(x, to, c, z), device(x, y, c, to), device(to, y, c, z))[k]
            self.copy(self.r.at[k, me], self.r.at[k, me], k + 1, dev).start()
        return None

    def finish(self):
        for k in range(4):
            self.stage(k).wait_send()


READY = ((0, 1), (2, 3, 4), (5, 6, 7))
TILE_A = (0, 1, 2, 3, 3, 0, 1, 2)


class TileReduction:
    @staticmethod
    def scratch():
        dma = pltpu.SemaphoreType.DMA
        return [
            VM((4, NZ, 144, 128), BF16), VM((3, NZ, 144, 128), BF16), VM((NZ, 144, 128), BF16),
            VM((3, 144, 128), BF16), VM((4, 144, 128), BF16), dma((5,)), dma((8,)),
        ]

    def __init__(self, own, fin, bufs):
        self.own, self.fin = own, fin
        self.rc, self.r1, self.s1, self.r2, self.r3, self.ss, self.rs = bufs
        self.x, self.y, self.c, self.z = place()
        self.flip = self.c == 1
        self.a, self.b = jnp.where(self.flip, self.y, self.x), jnp.where(self.flip, self.x, self.y)
        last = jnp.where(self.a == 3, 4, 5 + self.a)
        self.tile = jnp.where(self.c == lax.rem(self.a + 1, 2), self.a, last)

    def at(self, a, b, z, core=None):
        core = self.c if core is None else core
        return device(jnp.where(self.flip, b, a), jnp.where(self.flip, a, b), core, z)

    def whole(self, ref, k):
        return remote(
            ref, ref, self.ss.at[k], self.rs.at[3 + k], device(self.x, self.y, 1 - self.c, self.z))

    def core_copy(self, t):
        return remote(
            self.own.at[t], self.rc.at[t // 2], self.ss.at[0], self.rs.at[t // 2],
            device(self.x, self.y, 1 - self.c, self.z))

    def core_start(self, tiles):
        for t in tiles:

            @pl.when(self.c == t % 2)
            def _(t=t):
                self.core_copy(t).start()

    def core_add(self, tiles):
        for t in tiles:

            @pl.when(self.c != t % 2)
            def _(t=t):
                self.core_copy(t).wait_recv()
                for j in range(NZ):
                    self.own[t, j] = self.own[t, j] + self.rc[t // 2, j]

    def first_start(self, tiles):
        for t in tiles:
            to = TILE_A[t]

            @pl.when(jnp.logical_and(self.c != t % 2, self.a != to))
            def _(t=t, to=to):
                k = jnp.maximum(wrap(to + NX - self.a, NX) - 1, 0)
                remote(
                    self.own.at[t], self.r1.at[k], self.ss.at[1], self.rs.at[4],
                    self.at(to, self.b, self.z)).start()

    def first_sum(self):
        self.whole(self.r1, 1).wait_recv()
        for j in range(NZ):
            total = self.own[self.tile, j].astype(F32) + self.r1[0, j].astype(F32)
            total = total + self.r1[1, j].astype(F32) + self.r1[2, j].astype(F32)
            self.s1[j] = total.astype(BF16)

    def z_start(self):
        for d in range(1, NZ):
            to = wrap(self.z + d, NZ)
            remote(
                self.s1.at[to], self.r2.at[d - 1], self.ss.at[2], self.rs.at[5],
                device(self.x, self.y, self.c, to)).start()

    def z_sum(self):
        self.whole(self.r2, 2).wait_recv()
        total = self.s1[self.z].astype(F32) + self.r2[0].astype(F32)
        total = total + self.r2[1].astype(F32) + self.r2[2].astype(F32)
        self.r3[self.b] = total.astype(BF16)

    def exchange_start(self):
        ref = self.r3.at[self.b]
        for d in range(1, NY):
            remote(ref, ref, self.ss.at[3], self.rs.at[6],
                   self.at(self.a, wrap(self.b + d, NY), self.z)).start()

    def gather_start(self):
        self.whole(self.r3.at[0:3], 3).wait_recv()
        total = self.r3[0].astype(F32) + self.r3[1].astype(F32)
        total = total + self.r3[2].astype(F32) + self.r3[3].astype(F32)
        where = (slice(None), pl.ds(pl.multiple_of(self.tile * 128, 128), 128))
        self.fin[where] = total.astype(BF16)
        ref = self.fin.at[where]
        for e in range(2):
            for d in range(NX):
                if e or d:
                    remote(ref, ref, self.ss.at[4], self.rs.at[7],
                           self.at(wrap(self.a + d, 4), self.b, self.z, wrap(self.c + e, 2))).start()

    def gather_wait(self):
        self.whole(self.fin.at[:, 0:896], 4).wait_recv()

    def finish(self):
        for ref, k in (
            (self.rc, 0), (self.r1, 1), (self.r2, 2), (self.r3.at[0:3], 3), (self.fin.at[:, 0:896], 4),
        ):
            self.whole(ref, k).wait_send()


def step_kernel(
    tok_hbm, cot_hbm, cos_hbm, sin_hbm, vstates, states,
    block_out, grad_in, new_states, new_vectors, wgu_all, wdn_all, s,
):
    x, y, c, z = place()
    sib = device(x, y, 1 - c, z)
    zdev = [device(x, y, c, wrap(z + d, NZ)) for d in range(1, NZ)]
    xdev = [device(wrap(x + d, NX), y, c, z) for d in range(1, NX)]
    ydev = [device(x, wrap(y + d, NY), c, z) for d in range(1, NY)]
    peers = [sib] + xdev + ydev + zdev
    for d in range(1, 4):
        peers.append(device(wrap(x + d, NX), y, 1 - c, z))
        peers.append(device(x, wrap(y + d, NY), 1 - c, z))
    barrier = pltpu.get_barrier_semaphore()
    for peer in peers:
        pl.semaphore_signal(barrier, inc=1, device_id=peer, device_id_type=MESH)
    wq_v, vec_v, q_s, qt_s, kvs = s["wq"], s["vec"], s["q"], s["qt"], s["kv"]
    wo_all, b_gu, b_dn, n1t = s["wo"], s["ggu"].at[0, 0:2], s["gdn"].at[0, 0:2], s["n1t"]
    m_s, l_s, ot_s, lse, att = s["m"], s["l"], s["ot"], s["lse"], s["att"]
    loc_sem = s["loc"]
    row0 = pl.multiple_of(z * ROWS, ROWS)
    loads = [
        pltpu.make_async_copy(cos_hbm.at[pl.ds(row0, ROWS)], s["cos"], loc_sem.at[0]),
        pltpu.make_async_copy(sin_hbm.at[pl.ds(row0, ROWS)], s["sin"], loc_sem.at[1]),
        pltpu.make_async_copy(cot_hbm, s["n2t"], loc_sem.at[2]),
    ]
    masters = new_states[0]
    master_loads = [
        pltpu.make_async_copy(states[0][k], masters[k], s["st_sem"].at[0, k]) for k in range(4)]
    tok_t = s["tok"]
    tok_load = pltpu.make_async_copy(tok_hbm, tok_t, loc_sem.at[7])
    vector_loads = [
        pltpu.make_async_copy(vstates[i], new_vectors[i], s["v_sem"].at[i]) for i in range(3)]
    for load in vector_loads[0:1] + master_loads[0:1] + [tok_load] + master_loads[1:] + vector_loads[1:] + loads:
        load.start()
    vec_v[0] = jnp.zeros((1, VW), F32)
    vector_loads[0].wait()
    vec_v[0, :, 0:528] = new_vectors[0][...].reshape(1, 528)
    rolled = pltpu.roll(jnp.broadcast_to(vec_v[0], (8, VW)), z * 528, 1)
    vec_v[0] = rolled[0:1, :]
    qrows = pl.ds(pl.multiple_of(z * 144, 144), 144)
    master_loads[0].wait()
    wq_v[qrows, 0:896] = masters[0][:, 0:896].astype(BF16)
    wq_v[qrows, 896:1024] = jnp.concatenate(
        [masters[0][:, 896:960].astype(BF16), jnp.zeros((144, 64), BF16)], axis=1
    )
    pl.semaphore_wait(barrier, len(peers))

    sent = []

    def group(copies, name, shape):
        whole = remote(shape, shape, s["ss"].at[name], s["rs"].at[name], sib)
        return copies, whole

    def pair_of(name):
        return s["ss"].at[name], s["rs"].at[name]

    def begin(batch):
        for copy in batch[0]:
            copy.start()
        sent.append(batch[1])

    kcols = pl.ds(pl.multiple_of(512 + c * 256, 256), 256)
    xcols = pl.ds(pl.multiple_of(x * 128, 128), 128)
    ref_k, ref_q = wq_v.at[qrows, kcols], wq_v.at[qrows, xcols]
    k_over_z = group([remote(ref_k, ref_k, *pair_of(0), dev) for dev in zdev], 0, wq_v.at[0:432, 0:256])
    v_over_z = group(
        [remote(vec_v.at[0], vec_v.at[d], *pair_of(1), zdev[d - 1]) for d in range(1, NZ)], 1, vec_v.at[1:4])
    q_over_z = group([remote(ref_q, ref_q, *pair_of(2), dev) for dev in zdev], 2, wq_v.at[0:432, 0:128])
    begin(k_over_z)
    begin(v_over_z)

    @pl.when(c == 0)
    def _():
        for copy in q_over_z[0]:
            copy.start()

    def block_rows(e, n):
        return pl.ds(pl.multiple_of(wrap(z + NZ - e, NZ) * n, n), n)

    tok_load.wait()
    inputs = jnp.transpose(tok_t[...].astype(F32))
    s["gh"][...] = inputs
    unit = inputs * lax.rsqrt(jnp.mean(inputs * inputs, axis=-1, keepdims=True) + EPS)

    master_loads[1].wait()
    wo_all[qrows, 0:512] = masters[1][:, 0:512].astype(BF16)
    wo_all[qrows, 512:640] = jnp.concatenate(
        [masters[1][:, 512:576].astype(BF16), jnp.zeros((144, 64), BF16)], axis=1)
    own = []
    master_loads[2].wait()
    master_loads[3].wait()
    down = jnp.transpose(masters[3][...]).astype(BF16)
    zrows = pl.ds(pl.multiple_of(z * 384, 384), 384)
    for p in range(8):
        b_gu[p // 4, p % 4] = masters[2][:, 384 * p : 384 * p + 384].astype(BF16)
        b_dn[p // 4, p % 4] = down[48 * p : 48 * p + 48, :]
        own.append(
            pltpu.make_async_copy(
                b_gu.at[p // 4, p % 4], wgu_all.at[qrows, 384 * p : 384 * p + 384], loc_sem.at[5]))
        own.append(
            pltpu.make_async_copy(
                b_dn.at[p // 4, p % 4], wdn_all.at[pl.ds(pl.multiple_of(z * 384 + 48 * p, 48), 48), :],
                loc_sem.at[6]))
    own_done = [
        pltpu.make_async_copy(wgu_all.at[qrows, :], wgu_all.at[qrows, :], loc_sem.at[5]),
        pltpu.make_async_copy(wdn_all.at[zrows, :], wdn_all.at[zrows, :], loc_sem.at[6]),
    ]
    for copy in own:
        copy.start()

    w = wrap(x + y, 4)
    pgu = pl.multiple_of((c * 4 + w) * 384, 128)
    pdn = (c * 4 + y) * 48
    po = jnp.minimum(c * 4 + y, 4)
    has_o = c * 4 + y < 5
    oc = pl.multiple_of(po * 128, 128)

    def down_rows(zz):
        return wdn_all.at[pl.ds(pl.multiple_of(zz * 384 + pdn, 48), 48), :]

    o_over_z = group(
        [remote(wo_all.at[qrows, pl.ds(oc, 128)], wo_all.at[qrows, pl.ds(oc, 128)], *pair_of(3), dev) for dev in zdev],
        3, wo_all.at[0:432, 0:128])
    gu_over_z = group(
        [remote(b_gu.at[c, w], wgu_all.at[qrows, pl.ds(pgu, 384)], *pair_of(4), dev) for dev in zdev],
        4, wgu_all.at[0:432, 0:384])
    dn_over_z = group(
        [remote(b_dn.at[c, y], down_rows(z), *pair_of(5), dev) for dev in zdev], 5, wdn_all.at[0:144, :])

    def weights_over_z():
        @pl.when(has_o)
        def _():
            for copy in o_over_z[0]:
                copy.start()

        for copy in dn_over_z[0] + gu_over_z[0]:
            copy.start()

    weights_over_z()
    k_over_z[1].wait_recv()
    v_over_z[1].wait_recv()
    others = range(1, NZ)
    k_over_c = group(
        [remote(wq_v.at[block_rows(e, 144), kcols], wq_v.at[block_rows(e, 144), kcols], *pair_of(6), sib)
         for e in others], 6, wq_v.at[0:432, 0:256])
    begin(k_over_c)

    q_over_x = group(
        [remote(wq_v.at[block_rows(e, 144), xcols], wq_v.at[block_rows(e, 144), xcols], *pair_of(7), dev)
         for e in others for dev in xdev], 7, wq_v.at[0:432, 0:384])
    q_over_c = group(
        [remote(wq_v.at[block_rows(e, 144), 0:512], wq_v.at[block_rows(e, 144), 0:512], *pair_of(8), sib)
         for e in others], 8, wq_v.at[0:432, 0:512])

    @pl.when(c == 0)
    def _():
        q_over_z[1].wait_recv()
        for copy in q_over_x[0]:
            copy.start()

    raw = vec_v[0] + vec_v[1] + vec_v[2] + vec_v[3]
    raw = raw.astype(BF16).astype(F32)
    wide = jnp.broadcast_to(raw, (8, VW))
    gain_one = raw[:, 0:576]
    gain_two = pltpu.roll(wide, VW - 576, 1)[0:1, 0:576]
    bias = raw[:, 1152:2176]
    normed = unit * gain_one
    n1 = normed.astype(BF16)
    n1t[...] = jnp.transpose(normed).astype(BF16)
    for load in loads:
        load.wait()
    cosine, sine = s["cos"][...], s["sin"][...]

    k_over_c[1].wait_recv()

    def tile_of(v, t):
        return v[:, 128 * t : 128 * t + 128]

    def rotated(v):
        return v * cosine + swap_halves(v) * sine

    def turn(v):
        return pltpu.roll(v, 64, 1)

    proj = dot(n1, wq_v[:, 512:1024]) + bias[:, 512:1024]
    rot4, rot5 = rotated(tile_of(proj, 0)), rotated(tile_of(proj, 1))
    val6, val7 = tile_of(proj, 2), tile_of(proj, 3)
    low = low_lanes(rot4)
    kvs[z, 0] = jnp.where(low, turn(rot4), turn(val6)).astype(BF16)
    kvs[z, 1] = jnp.where(low, rot5, val6).astype(BF16)
    kvs[z, 2] = jnp.where(low, turn(rot5), turn(val7)).astype(BF16)
    kv_sends = []
    for d in range(1, NZ):
        kv_sends.append(
            remote(kvs.at[z], kvs.at[z], s["kv_s"].at[d - 1], s["kv_r"].at[d - 1],
                   device(x, y, c, wrap(z + d, NZ))))

        @pl.when(z + d < NZ)
        def _(d=d):
            kv_sends[d - 1].start()

    def put_query(h, part):
        qh = jnp.where(low, part, 0.0) * (HEAD_DIM ** -0.5)
        q_s[h] = qh.astype(BF16)
        qt_s[h] = jnp.transpose(qh).astype(BF16)

    put_query(8, rot4)
    s["cot"][...] = jnp.transpose(s["n2t"][...].astype(F32)).astype(BF16)

    @pl.when(c == 0)
    def _():
        q_over_x[1].wait_recv()
        for copy in q_over_c[0]:
            copy.start()

    @pl.when(c == 1)
    def _():
        q_over_c[1].wait_recv()

    proj = dot(n1, wq_v[:, 0:512]) + bias[:, 0:512]
    for t in range(4):
        rot = rotated(tile_of(proj, t))
        put_query(2 * t, rot)
        put_query(2 * t + 1, turn(rot))

    def step(j):
        kvt = [jnp.transpose(kvs[j, g].astype(F32)).astype(BF16)[64:128, :] for g in range(KV_HEADS)]
        heads = range(HEADS)
        sts = [dot(kvs[j, h // GROUP], qt_s[h]) for h in heads]
        olds = [m_s[h] for h in heads]
        peaks = [jnp.maximum(jnp.max(v, axis=0, keepdims=True), o) for v, o in zip(sts, olds)]
        alphas = [jnp.exp(o - p) for o, p in zip(olds, peaks)]
        ps = [jnp.exp(v - p) for v, p in zip(sts, peaks)]
        totals = [jnp.sum(p, axis=0, keepdims=True) + l_s[h] * a for h, p, a in zip(heads, ps, alphas)]
        outs = [dot(kvt[h // GROUP], p.astype(BF16)) + ot_s[h] * a for h, p, a in zip(heads, ps, alphas)]
        for h in heads:
            m_s[h] = peaks[h]
            l_s[h] = totals[h]
            ot_s[h] = outs[h]

    def visible(width):
        shape = (256, width)
        return lax.broadcasted_iota(jnp.int32, shape, 0) <= lax.broadcasted_iota(jnp.int32, shape, 1)

    right = slice(256, 512)
    always = z >= 0

    @pl.when(always)
    def _():
        keep_a, keep_b = visible(512), visible(256)
        kvt = [jnp.transpose(kvs[z, g].astype(F32)).astype(BF16)[64:128, :] for g in range(KV_HEADS)]
        heads = range(HEADS)
        st_a = [jnp.where(keep_a, dot(kvs[z, h // GROUP, 0:256], qt_s[h]), MASK_FILL) for h in heads]
        st_b = [jnp.where(keep_b, dot(kvs[z, h // GROUP, right], qt_s[h, :, right]), MASK_FILL) for h in heads]
        none = jnp.full((1, 256), MASK_FILL, F32)
        zero = jnp.zeros((1, 256), F32)
        zeros = jnp.zeros((64, 256), F32)
        peaks = [
            jnp.maximum(
                jnp.max(a, axis=0, keepdims=True),
                jnp.concatenate([none, jnp.max(b, axis=0, keepdims=True)], axis=1))
            for a, b in zip(st_a, st_b)]
        p_a = [jnp.exp(a - p) for a, p in zip(st_a, peaks)]
        p_b = [jnp.exp(b - p[:, right]) for b, p in zip(st_b, peaks)]
        totals = [
            jnp.sum(a, axis=0, keepdims=True) + jnp.concatenate([zero, jnp.sum(b, axis=0, keepdims=True)], axis=1)
            for a, b in zip(p_a, p_b)]
        outs = [
            dot(kvt[h // GROUP][:, 0:256], p_a[h].astype(BF16))
            + jnp.concatenate([zeros, dot(kvt[h // GROUP][:, right], p_b[h].astype(BF16))], axis=1)
            for h in heads]
        for h in heads:
            m_s[h] = peaks[h]
            l_s[h] = totals[h]
            ot_s[h] = outs[h]

    gu_over_z[1].wait_recv()
    dn_over_z[1].wait_recv()

    @pl.when(has_o)
    def _():
        o_over_z[1].wait_recv()

    def gu_piece(e, ww):
        return wgu_all.at[block_rows(e, 144), pl.ds(pl.multiple_of((c * 4 + ww) * 384, 128), 384)]

    def o_piece(e):
        return wo_all.at[block_rows(e, 144), pl.ds(oc, 128)]

    def dn_half(e):
        return wdn_all.at[
            pl.ds(pl.multiple_of(wrap(z + NZ - e, NZ) * 384 + c * 192, 192), 192), :]

    def dn_piece(e):
        return down_rows(wrap(z + NZ - e, NZ))

    gu_over_x = group(
        [remote(gu_piece(e, w), gu_piece(e, w), *pair_of(9), dev) for e in others for dev in xdev],
        9, wgu_all.at[0:432, 0:1152])
    dn_over_y = group(
        [remote(dn_piece(e), dn_piece(e), *pair_of(10), dev) for e in others for dev in ydev],
        10, wdn_all.at[0:432, :])
    o_over_y = [
        [remote(o_piece(e), o_piece(e), s["ss"].at[11], s["os"].at[d - 1], ydev[d - 1]) for e in others]
        for d in range(1, NY)]
    o_sent = remote(wo_all.at[0:432, 0:384], wo_all.at[0:432, 0:384], s["ss"].at[11], s["os"].at[0], sib)
    own_over_c = group(
        [remote(gu_piece(e, w), gu_piece(e, w), *pair_of(12), sib) for e in others], 12, wgu_all.at[0:432, 0:384])
    gu_over_c = group(
        [remote(gu_piece(e, wrap(w + d, NX)), gu_piece(e, wrap(w + d, NX)), *pair_of(13), sib)
         for e in others for d in range(1, NX)], 13, wgu_all.at[0:432, 0:1152])
    dn_over_c = group(
        [remote(dn_half(e), dn_half(e), *pair_of(14), sib) for e in others], 14, wdn_all.at[0:576, :])
    o_over_c = []
    for core, cols in enumerate((slice(0, 512), slice(512, 640))):
        o_over_c.append(
            group(
                [remote(wo_all.at[block_rows(e, 144), cols], wo_all.at[block_rows(e, 144), cols], *pair_of(15), sib)
                 for e in others], 15, wo_all.at[0:432, cols]))

    @pl.when(has_o)
    def _():
        for copies in o_over_y:
            for copy in copies:
                copy.start()

    begin(dn_over_y)
    begin(gu_over_x)
    begin(own_over_c)

    def earlier(d, carry):
        @pl.when(d == NZ - 1)
        def _():
            for dd in range(1, NY):
                from_y = wrap(y + NY - dd, NY)

                @pl.when(c * 4 + from_y < 5)
                def _(dd=dd):
                    remote(wo_all.at[0:432, 0:128], wo_all.at[0:432, 0:128], s["ss"].at[11], s["os"].at[dd - 1],
                           sib).wait_recv()

            for core in range(2):

                @pl.when(c == core)
                def _(core=core):
                    for copy in o_over_c[core][0]:
                        copy.start()

            dn_over_y[1].wait_recv()
            begin(dn_over_c)

        @pl.when(z >= d)
        def _():
            remote(kvs.at[z], kvs.at[z], s["kv_s"].at[d - 1], s["kv_r"].at[d - 1], sib).wait_recv()
            step(z - d)

        return carry

    lax.fori_loop(1, NZ, earlier, 0)

    for h in range(HEADS):
        ot_s[h] = ot_s[h] * (1.0 / l_s[h])
        lse[h] = m_s[h] + jnp.log(l_s[h])
    for t in range(5):
        top = ot_s[2 * t]
        bottom = ot_s[2 * t + 1] if 2 * t + 1 < HEADS else jnp.zeros((64, ROWS), F32)
        att[:, 128 * t : 128 * t + 128] = jnp.transpose(jnp.concatenate([top, bottom], axis=0)).astype(BF16)

    for core in range(2):

        @pl.when(c == core)
        def _(core=core):
            o_over_c[1 - core][1].wait_recv()

    for copy in own_done:
        copy.wait()
    wo = wo_all
    wgu, wds, w_sem = s["wgu"], s["wds"], s["w_sem"]

    def weights(i, slot):
        col = pl.multiple_of(wrap(w + i, 4) * 384, 384)
        return [
            pltpu.make_async_copy(
                wgu_all.at[:, pl.ds(col, 384)], wgu.at[slot, :, 0:384], w_sem.at[0, slot]),
            pltpu.make_async_copy(
                wgu_all.at[:, pl.ds(pl.multiple_of(col + FF, 384), 384)], wgu.at[slot, :, 384:768],
                w_sem.at[0, slot]),
            pltpu.make_async_copy(wdn_all.at[pl.ds(col, 384), :], wds.at[slot], w_sem.at[1, slot]),
        ]

    def weights_wait(slot):
        pltpu.make_async_copy(wgu_all.at[:, 0:768], wgu.at[slot], w_sem.at[0, slot]).wait()
        pltpu.make_async_copy(wdn_all.at[0:384, :], wds.at[slot], w_sem.at[1, slot]).wait()

    gu_over_z[1].wait_send()
    dn_over_z[1].wait_send()
    dn_over_c[1].wait_recv()
    own_over_c[1].wait_recv()
    for load in weights(0, 0):
        load.start()
    gu_over_x[1].wait_recv()
    begin(gu_over_c)

    ggu, gdn, go, gq, fin = s["ggu"], s["gdn"], s["go"], s["gq"], s["fin"]
    def columns(width):
        def at(cc, a, count):
            return (slice(None), pl.ds(pl.multiple_of((cc * 4 + a) * width, 128), count * width))

        return at

    def down_at(cc, a, count):
        return (pl.ds(pl.multiple_of((cc * 4 + a) * 48, 48), count * 48), slice(None))

    red_gu = Reduction(ggu, fin["gu"], columns(384), s["red_gu"], 0, False)
    red_dn = Reduction(gdn, fin["dn"], down_at, s["red_dn"], 1, True)
    red_o = Reduction(go, fin["o"], columns(128), s["red_o"], 0, False)
    red_q = TileReduction(gq, fin["q"], s["red_q"])
    vecs = VectorSum(s["vecs"])
    cot, gh, n2, n2t, gn2t = s["cot"], s["gh"], s["n2"], s["n2t"], grad_in
    do_in, dot_in, delta_in, gain_row = s["do"], s["dot"], s["delta"], s["gain_row"]
    dqt, own_kv, skv, rkv = ot_s, s["own_kv"], s["skv"], s["rkv"]

    gn2t[...] = jnp.zeros_like(gn2t)
    hid = gh[...] + dot(att[:, 0:576], wo[:, 0:576])
    inv_two = lax.rsqrt(jnp.mean(hid * hid, axis=-1, keepdims=True) + EPS)
    normed = hid * inv_two * gain_two
    n2[...] = normed.astype(BF16)
    n2t[...] = jnp.transpose(normed).astype(BF16)
    gh[...] = hid
    block_out[...] = jnp.transpose(hid)

    def chunk(i, carry):
        slot = lax.rem(i, 2)
        here = wrap(w + i, 4)
        @pl.when(i > 0)
        def _():
            red_gu.core_add(wrap(w + i + 3, 4))
            red_gu.first_piece(wrap(w + i + 3, 4))

        weights_wait(slot)

        @pl.when(jnp.logical_and(i > 0, i < 3))
        def _():
            for load in weights(i + 1, 1 - slot):
                load.start()

        both = dot(n2[...], wgu[slot])
        gate, up = both[:, 0:384], both[:, 384:768]
        sg = jax.nn.sigmoid(gate)
        silu = gate * sg
        act = (silu * up).astype(BF16)
        ga = dot(cot[...], wds[slot], 1, 1)
        gg = (ga * up * sg * (1.0 + gate * (1.0 - sg))).astype(BF16)
        gu = (ga * silu).astype(BF16)
        grads = jnp.concatenate([gg, gu], axis=1)
        both = dot(n2t[...], grads).astype(BF16)
        ggu[0, here] = both[:, 0:384].reshape(NZ, 144, 384)
        ggu[1, here] = both[:, 384:768].reshape(NZ, 144, 384)
        red_gu.core_copy(here).start()
        down = dot(act, cot[...], 0, 0).astype(BF16)
        for p in range(8):
            gdn[p // 4, here, p % 4] = down[48 * p : 48 * p + 48, :]
        red_dn.core_copy(here).start()

        @pl.when(i == 0)
        def _():
            gu_over_c[1].wait_recv()
            for load in weights(1, 1):
                load.start()

        block_out[...] += lax.dot_general(wds[slot], act, (((0,), (1,)), ((), ())), preferred_element_type=F32)
        gn2t[...] += dot(wgu[slot], grads, 1, 1)

        return carry

    lax.fori_loop(0, 4, chunk, 0)

    red_gu.core_add(wrap(w + 3, 4))
    red_gu.first_piece(wrap(w + 3, 4))
    state_loads = []
    for i in range(1, 3):
        for k in range(4):
            copy = pltpu.make_async_copy(states[i][k], new_states[i][k], s["st_sem"].at[i, k])
            copy.start()
            state_loads.append(copy)

    @pl.when(always)
    def _():
        hid = gh[...]
        inv_two = lax.rsqrt(jnp.mean(hid * hid, axis=-1, keepdims=True) + EPS)
        u = hid * inv_two
        e = jnp.transpose(gn2t[...])
        f = e * gain_two
        gain_row[:, 0:576] = jnp.sum(e * u, axis=0, keepdims=True)
        gain_row[:, 576:640] = jnp.zeros((1, 64), F32)
        grad_hidden = cot[...].astype(F32) + inv_two * (f - u * jnp.mean(f * u, axis=-1, keepdims=True))
        gh[...] = grad_hidden
        ghl = grad_hidden.astype(BF16)
        grad_out = dot(att[:, 0:576], ghl, 0, 0).astype(BF16)
        for p in range(8):
            if p < 4:
                part = grad_out[:, 128 * p : 128 * p + 128]
            elif p == 4:
                part = jnp.concatenate([grad_out[:, 512:576], jnp.zeros((D, 64), BF16)], axis=1)
            else:
                part = jnp.zeros((D, 128), BF16)
            go[p // 4, p % 4] = part.reshape(NZ, 144, 128)
        red_o.core_all(lambda k: red_o.core_copy(k).start())
        gm = dot(ghl, wo[:, 0:576], 1, 1).astype(BF16).astype(F32)
        gm = jnp.concatenate([gm, jnp.zeros((ROWS, 64), F32)], axis=1)
        for h in range(HEADS):
            part = gm[:, 128 * (h // 2) : 128 * (h // 2) + 128]
            part = part if h % 2 == 1 else turn(part)
            part = jnp.where(low_lanes(part), 0.0, part)
            do_in[h] = part.astype(BF16)
            part = jnp.transpose(part)
            dot_in[h] = part.astype(BF16)
            delta_in[h] = jnp.sum(part[64:128, :] * ot_s[h], axis=0, keepdims=True)

    red_dn.core_all(red_dn.core_add)
    red_dn.first_start()

    def attend(g, j):
        kv = kvs[j, g]
        kt = jnp.transpose(kv.astype(F32)).astype(BF16)[0:64, :]
        totals = [None, None]
        for i in range(GROUP):
            h = g * GROUP + i
            dq = None
            for half in range(2):
                rows = slice(256 * half, 256 * half + 256)
                pt = jnp.exp(dot(kv[rows], qt_s[h]) - lse[h])
                dst = (pt * (dot(kv[rows], dot_in[h]) - delta_in[h])).astype(BF16)
                both = dot(dst, q_s[h]) + dot(pt.astype(BF16), do_in[h])
                totals[half] = both if i == 0 else totals[half] + both
                part = dot(kt[:, rows], dst)
                dq = part if half == 0 else dq + part
            dqt[h] += dq
        return totals

    def attend_own(g):
        keep_a, keep_b = visible(512), visible(256)
        kv = kvs[z, g]
        kt = jnp.transpose(kv.astype(F32)).astype(BF16)[0:64, :]
        left = slice(0, 256)
        totals = [None, None]
        for i in range(GROUP):
            h = g * GROUP + i
            pt = jnp.where(keep_a, jnp.exp(dot(kv[left], qt_s[h]) - lse[h]), 0.0)
            dst = (pt * (dot(kv[left], dot_in[h]) - delta_in[h])).astype(BF16)
            both = dot(dst, q_s[h]) + dot(pt.astype(BF16), do_in[h])
            totals[0] = both if i == 0 else totals[0] + both
            dq = dot(kt[:, left], dst)
            pt = jnp.where(keep_b, jnp.exp(dot(kv[right], qt_s[h, :, right]) - lse[h, :, right]), 0.0)
            dst = (pt * (dot(kv[right], dot_in[h, :, right]) - delta_in[h, :, right])).astype(BF16)
            both = dot(dst, q_s[h, right]) + dot(pt.astype(BF16), do_in[h, right])
            totals[1] = both if i == 0 else totals[1] + both
            dqt[h] += dq
            dqt[h, :, right] += dot(kt[:, right], dst)
        own_kv[g, left] = totals[0]
        own_kv[g, right] = totals[1]

    def kv_copy(g, k, dev):
        return remote(
            skv.at[g, k - 1], rkv.at[g, k - 1], s["ss"].at[16], s["dkv_r"].at[g], dev)

    gps = q_s

    def kv_wait(g):
        for count in range(1, NZ):

            @pl.when(z + count == NZ - 1)
            def _(count=count):
                part = rkv.at[g, 0:count]
                remote(part, part, s["ss"].at[16], s["dkv_r"].at[g], sib).wait_recv()
                total = own_kv[g]
                for k in range(count):
                    total = total + rkv[g, k].astype(F32)
                own_kv[g] = total

    def group_tiles(g):
        cos_t, sin_t = s["cos"][...], s["sin"][...]
        low = low_lanes(cos_t)
        kv = own_kv[g]

        def query(top, bottom):
            both = [dqt[h] if h is not None else jnp.zeros((64, ROWS), F32) for h in (top, bottom)]
            return jnp.transpose(jnp.concatenate(both, axis=0)) * (HEAD_DIM ** -0.5)

        def back(t):
            return t * cos_t - swap_halves(t) * sin_t

        if g == 0:
            return {
                0: back(query(0, 1)),
                1: back(jnp.where(low, query(2, None), turn(kv))),
                2: jnp.where(low, turn(kv), 0.0),
            }
        if g == 1:
            return {
                2: jnp.where(low, 0.0, back(query(None, 3))),
                3: back(query(4, 5)),
                4: jnp.where(low, back(kv), kv),
            }
        return {
            5: back(query(6, 7)),
            6: back(jnp.where(low, query(8, None), turn(kv))),
            7: jnp.where(low, turn(kv), 0.0),
        }

    def tiles_of(g):
        @pl.when(always)
        def _():
            for t, tile in group_tiles(g).items():
                if t == 2 and g == 0:
                    gps[2] = tile.astype(BF16)
                    continue
                if t == 2:
                    tile = tile + gps[2].astype(F32)
                low_tile = tile.astype(BF16)
                gps[t] = low_tile
                gq[t] = dot(n1t[...], low_tile).astype(BF16).reshape(NZ, 144, 128)

        red_q.core_start((READY[g]))

    dqt[...] = jnp.zeros_like(dqt)
    early = red_q.tile <= 4
    late = red_q.tile > 4
    own_one = jnp.where(z == NZ - 1, 9, 3)
    own_two = jnp.where(z == NZ - 1, 10, 6)

    def slot(t, carry):
        g = lax.div(t, 3)
        k = 3 - lax.rem(t, 3)

        @pl.when(jnp.logical_and(t < 9, z >= k))
        def _():
            for half, total in enumerate(attend(g, z - k)):
                skv[g, k - 1, 256 * half : 256 * half + 256] = total.astype(BF16)
            kv_copy(g, k, device(x, y, c, z - k)).start()

        @pl.when(jnp.logical_or(t == 2, jnp.logical_or(t == own_one, t == own_two)))
        def _():
            attend_own(jnp.where(t == 2, 0, jnp.where(t == own_one, 1, 2)))

        @pl.when(t == 0)
        def _():
            red_o.core_all(red_o.core_add)

        @pl.when(t == 2)
        def _():
            red_gu.first_sum()
            red_gu.z_start()
            red_o.first_start()

        @pl.when(t == 4)
        def _():
            kv_wait(0)
            tiles_of(0)

        @pl.when(t == 5)
        def _():
            red_q.core_add(READY[0])
            red_q.first_start(READY[0])
            red_gu.z_sum()
            red_gu.exchange_start()

        @pl.when(t == 9)
        def _():
            kv_wait(1)
            tiles_of(1)
            red_dn.first_sum()
            red_o.first_sum()
            red_q.core_add(READY[1])
            red_q.first_start(READY[1])
            red_gu.gather_start()

        return carry

    lax.fori_loop(0, 11, slot, 0)
    kv_wait(2)
    red_dn.z_start()
    red_o.z_start()
    tiles_of(2)
    red_q.core_add(READY[2])
    red_q.first_start(READY[2])

    low = low_lanes(s["cos"][...])

    def halves(t):
        tile = gps[t].astype(F32)
        return tile, turn(tile)

    (t0, _), (t1, u1), (t2, u2), (t3, u3) = [halves(t) for t in range(4)]
    (t4, u4), (t5, _), (t6, u6), (t7, _) = [halves(t) for t in range(4, 8)]
    ordered = [
        t0,
        jnp.where(low, t1, t2),
        t3,
        t5,
        jnp.where(low, t6, t1),
        jnp.where(low, t4, t6),
        jnp.where(low, t2, t4),
        t7,
    ]
    vecs.rc[0, 10:18, :] = jnp.concatenate(
        [jnp.sum(t, axis=0, keepdims=True) for t in ordered], axis=0)
    gn1 = dot(jnp.concatenate([t.astype(BF16) for t in ordered], axis=1), wq_v[...], 1, 1)
    inputs = jnp.transpose(tok_t[...].astype(F32))
    r = lax.rsqrt(jnp.mean(inputs * inputs, axis=-1, keepdims=True) + EPS)
    u = inputs * r
    f = gn1 * gain_one
    row = jnp.sum(gn1 * u, axis=0, keepdims=True)
    row = jnp.concatenate([row, jnp.zeros((1, 64), F32)], axis=1)
    for t in range(5):
        vecs.rc[0, t : t + 1, :] = row[:, 128 * t : 128 * t + 128]
        vecs.rc[0, 5 + t : 6 + t, :] = gain_row[:, 128 * t : 128 * t + 128]
    vecs.rc[0, 18:24, :] = jnp.zeros((6, 128), F32)
    vecs.start()
    vecs.next(0)
    @pl.when(early)
    def _():
        red_q.first_sum()
        red_q.z_start()

    grad_in[...] = jnp.transpose(gh[...] + r * (f - u * jnp.mean(f * u, axis=-1, keepdims=True)))

    def update(k, grad):
        new = adam_step(
            new_states[0][k][...], new_states[1][k][...], new_states[2][k][...], grad, RATE_MATRIX, DECAY_MATRIX)
        for i in range(3):
            new_states[i][k][...] = new[i]

    red_gu.gather_forward()
    @pl.when(late)
    def _():
        red_q.first_sum()
        red_q.z_start()

    vecs.next(1)
    red_dn.z_sum()
    red_dn.exchange_start()
    red_o.z_sum()
    red_o.exchange_start()

    @pl.when(early)
    def _():
        red_q.z_sum()
        red_q.exchange_start()

    @pl.when(late)
    def _():
        red_q.z_sum()
        red_q.exchange_start()

    red_dn.gather_start()
    red_o.gather_start()

    for load in state_loads:
        load.wait()
    red_gu.gather_wait()
    update(2, fin["gu"][...].astype(F32))
    @pl.when(early)
    def _():
        red_q.gather_start()

    vecs.next(2)

    @pl.when(late)
    def _():
        red_q.gather_start()

    red_dn.gather_forward()
    red_o.gather_forward()
    red_dn.gather_wait()
    update(3, jnp.transpose(fin["dn"][...].astype(F32)))
    red_o.gather_wait()
    update(1, fin["o"][:, 0:576].astype(F32))
    total = vecs.next(3)
    total = jnp.concatenate([total[t : t + 1, :] for t in range(18)], axis=1)
    pad = jnp.zeros((1, VW - 640), F32)
    flat = jnp.concatenate([total[:, 0:640], pad], axis=1)
    mid = jnp.concatenate([total[:, 640:1280], pad], axis=1)
    flat = flat + pltpu.roll(jnp.broadcast_to(mid, (8, VW)), 576, 1)[0:1, :]
    flat = flat + jnp.concatenate(
        [jnp.zeros((1, 1152), F32), total[:, 1280:2304], jnp.zeros((1, 128), F32)], axis=1)
    shift = lax.rem(VW - z * 528, VW)
    grad = pltpu.roll(jnp.broadcast_to(flat, (8, VW)), shift, 1)[0:1, 0:528]
    for load in vector_loads[1:]:
        load.wait()
    new = adam_step(*[v[...].reshape(1, 528) for v in new_vectors], grad, RATE_VECTOR, 0.0)
    for i in range(3):
        new_vectors[i][...] = new[i].reshape(528)
    red_q.gather_wait()
    tq = [fin["q"][:, 128 * t : 128 * t + 128].astype(F32) for t in range(8)]
    lowq = low_lanes(tq[0])
    ordered = [
        tq[0],
        jnp.where(lowq, tq[1], tq[2]),
        tq[3],
        tq[5],
        jnp.where(lowq, tq[6], tq[1]),
        jnp.where(lowq, tq[4], tq[6]),
        jnp.where(lowq, tq[2], tq[4]),
        tq[7],
    ]
    update(0, jnp.concatenate(ordered, axis=1)[:, 0:960])
    for red in (red_gu, red_dn, red_o):
        red.finish()
    red_q.finish()
    vecs.finish()
    for whole in sent:
        whole.wait_send()
    for count in range(1, NZ):

        @pl.when(z == count)
        def _(count=count):
            part = (skv.at[0], skv.at[0:2], skv)[count - 1]
            remote(part, part, s["ss"].at[16], s["dkv_r"].at[0], sib).wait_send()

    for d in range(1, NZ):

        @pl.when(z + d < NZ)
        def _(d=d):
            kv_sends[d - 1].wait_send()

    @pl.when(has_o)
    def _():
        o_over_z[1].wait_send()
        o_sent.wait_send()

    for core in range(2):

        @pl.when(c == core)
        def _(core=core):
            o_over_c[core][1].wait_send()

    @pl.when(c == 0)
    def _():
        for batch in (q_over_z, q_over_x, q_over_c):
            batch[1].wait_send()


MATRICES = ((144, 960), (144, D), (144, 2 * FF), (D, 384))


def train(tok_t, cot_t, cos_t, sin_t, vstates, states):
    sd = jax.ShapeDtypeStruct
    v = pl.BlockSpec(memory_space=VM)
    a = pl.BlockSpec(memory_space=ANY)
    dma = pltpu.SemaphoreType.DMA
    scratch = dict(
        wq=VM((D, QW), BF16), vec=VM((NZ, 1, VW), F32), cos=VM((ROWS, 128), F32), sin=VM((ROWS, 128), F32),

        q=VM((HEADS, ROWS, 128), BF16), qt=VM((HEADS, 128, ROWS), BF16), n1t=VM((D, ROWS), BF16),
        kv=VM((NZ, KV_HEADS, ROWS, 128), BF16),
        m=VM((HEADS, 1, ROWS), F32), l=VM((HEADS, 1, ROWS), F32), ot=VM((HEADS, 64, ROWS), F32),
        lse=VM((HEADS, 1, ROWS), F32), att=VM((ROWS, 640), BF16), wo=VM((D, OW), BF16),
        loc=dma((8,)), v_sem=dma((3,)), tok=VM((D, ROWS), BF16), ss=dma((17,)), rs=dma((16,)), os=dma((3,)), kv_s=dma((3,)), kv_r=dma((3,)),
        cot=VM((ROWS, D), BF16), gh=VM((ROWS, D), F32), n2=VM((ROWS, D), BF16), n2t=VM((D, ROWS), BF16),
        wgu=VM((2, D, 768), BF16), wds=VM((2, 384, D), BF16), w_sem=dma((2, 2)),
        do=VM((HEADS, ROWS, 128), BF16), dot=VM((HEADS, 128, ROWS), BF16), delta=VM((HEADS, 1, ROWS), F32),
        gain_row=VM((1, 640), F32),
        ggu=VM((2, 4, NZ, 144, 384), BF16), gdn=VM((2, NZ, 4, 48, D), BF16), go=VM((2, 4, NZ, 144, 128), BF16),
        gq=VM((8, NZ, 144, 128), BF16),
        fin=dict(gu=VM((144, 2 * FF), BF16), dn=VM((384, D), BF16), o=VM((144, QW), BF16), q=VM((144, QW), BF16)),
        own_kv=VM((KV_HEADS, ROWS, 128), F32),
        skv=VM((KV_HEADS, 3, ROWS, 128), BF16), rkv=VM((KV_HEADS, 3, ROWS, 128), BF16),
        dkv_r=dma((3,)), st_sem=dma((3, 4)),
        red_gu=Reduction.scratch((4, 4), 144, 384), red_dn=Reduction.scratch((4, 4), 48, D),
        red_o=Reduction.scratch((4, 4), 144, 128), red_q=TileReduction.scratch(),
        vecs=VectorSum.scratch(),
    )
    fast = lambda shape: VM(shape, F32)
    return pl.pallas_call(
        step_kernel,
        out_shape=(
            fast((D, ROWS)),
            fast((D, ROWS)),
            [[fast(shape) for shape in MATRICES] for _ in range(3)],
            [fast((528,)) for _ in range(3)],
            pltpu.HBM((D, 2 * FF), BF16),
            pltpu.HBM((FF, D), BF16),
        ),
        in_specs=[a, a, a, a, [a] * 3, [[a] * 4] * 3],
        out_specs=(v, v, [[v] * 4] * 3, [v] * 3, a, a),
        scratch_shapes=[scratch],
        compiler_params=pltpu.CompilerParams(
            collective_id=0, has_side_effects=True, vmem_limit_bytes=51 << 20),
        name="train_step",
    )(tok_t, cot_t, cos_t, sin_t, vstates, states)


def adam_step(weight, first_state, second_state, gradient, learn_rate, decay_rate):
    first_new = BETA_ONE * first_state + (1.0 - BETA_ONE) * gradient
    second_new = BETA_TWO * second_state + (1.0 - BETA_TWO) * gradient * gradient
    corr_one = 1.0 - BETA_ONE**STEP
    corr_two = 1.0 - BETA_TWO**STEP
    update = first_new / corr_one / (jnp.sqrt(second_new / corr_two) + ADAM_EPS)
    weight_new = weight - learn_rate * (update + decay_rate * weight)
    return (weight_new, first_new, second_new)


def store_kernel(sources, *rest):
    targets, sems = rest[:-1], rest[-1]
    copies = [
        pltpu.make_async_copy(a, b, sems.at[k])
        for k, (a, b) in enumerate(zip(jax.tree.leaves(sources), jax.tree.leaves(targets)))]
    for copy in copies:
        copy.start()
    for copy in copies:
        copy.wait()


def store(arrays):
    shapes = jax.tree.map(lambda t: jax.ShapeDtypeStruct(t.shape, t.dtype), arrays)
    count = len(jax.tree.leaves(arrays))
    v = pl.BlockSpec(memory_space=VM)
    a = pl.BlockSpec(memory_space=ANY)
    return pl.pallas_call(
        store_kernel,
        out_shape=shapes,
        in_specs=[jax.tree.map(lambda t: v, arrays)],
        out_specs=jax.tree.map(lambda t: a, arrays),
        scratch_shapes=[pltpu.SemaphoreType.DMA((count,))],
        compiler_params=pltpu.CompilerParams(vmem_limit_bytes=8 << 20),
        name="store",
    )(arrays)


def per_device(
    tokens, cotangent, w_qkv, w_out, w_gate_up, w_down, vectors,
    first_qkv, first_out, first_gate_up, first_down, first_vectors,
    second_qkv, second_out, second_gate_up, second_down, second_vectors,
):
    cos_np, sin_np = rope_tables()
    cos_t, sin_t = jnp.asarray(cos_np), jnp.asarray(sin_np)
    states = [
        [w_qkv, w_out, w_gate_up, w_down.T],
        [first_qkv, first_out, first_gate_up, first_down.T],
        [second_qkv, second_out, second_gate_up, second_down.T],
    ]
    vstates = [vectors, first_vectors, second_vectors]
    outs = train(
        tokens.T, cotangent.T, cos_t, sin_t, vstates, states)
    block_t, grad_t, matrices, vecs = store(tuple(outs[0:4]))
    out = [block_t.T, grad_t.T]
    for i in range(3):
        out += list(matrices[i][0:3]) + [matrices[i][3].T, vecs[i]]
    return tuple(out)


def solution(mesh):
    tokens = P(("dp", "ctx"), None)
    state = (P("ctx", None),) * 4 + (P("ctx"),)
    return jax.shard_map(
        per_device, mesh=mesh, in_specs=(tokens, tokens) + state * 3, out_specs=(tokens, tokens) + state * 3,
        check_vma=False,
    )
```

profile of v0, /device:TPU:1, one launch (start us, length us, event | category | flops | bytes accessed | tf_op | source)
XLA Modules:
  0.0 122.7 jit_solution(17338362248842162203)
XLA Ops:
  0.7 117.0 %train_step.1 = (f32[576,512]{1,0:T(8,128)S(1)}, f32[576,512]{1,0:T(8,128)S(1)}, f32[144,960]{1,0:T(8,128)S(1)}, f32[144,576]{1,0:T(8,128)S(1)}, f32[144,3072]{1...) custom-call(bf16[576,512]{1,0:T(8,128)(2,1)} %bitcast.13, ...), custom_call_target="tpu_custom_call" | custom-call | tf_op jit(solution)/shard_map/train_step/pallas_call | solution.py:1253
  117.6 4.9 %store.1 = (f32[576,512]{1,0:T(8,128)}, f32[576,512]{1,0:T(8,128)}, f32[144,960]{1,0:T(8,128)}, f32[144,576]{1,0:T(8,128)}, f32[144,3072]{1,0:T(8,128)}, /*index...) custom-call(f32[576,512]{1,0:T(8,128)S(1)} %get-tuple-element.51.sou, ...), custom_call_target="tpu_custom_call" | custom-call | tf_op jit(solution)/shard_map/store/pallas_call | solution.py:1298
where the time goes:
time: 123 us
  Pallas kernels  122 us (99%)
    pallas_call x1, Pallas kernels, train(): pl.pallas_call(step_kernel, out_shape=(fast((D, ROWS)), fast((D, ROWS)),...  117 us
    pallas_call x1, Pallas kernels, store(): pl.pallas_call(store_kernel, out_shape=shapes, in_specs=[jax.tree.map(lam...  4.94 us

commit v1 on v0

--- a/solution.py
+++ b/solution.py
@@ -623,6 +623,60 @@
     right = slice(256, 512)
     always = z >= 0
 
+    gu_over_z[1].wait_recv()
+    dn_over_z[1].wait_recv()
+
+    @pl.when(has_o)
+    def _():
+        o_over_z[1].wait_recv()
+
+    def gu_piece(e, ww):
+        return wgu_all.at[block_rows(e, 144), pl.ds(pl.multiple_of((c * 4 + ww) * 384, 128), 384)]
+
+    def o_piece(e):
+        return wo_all.at[block_rows(e, 144), pl.ds(oc, 128)]
+
+    def dn_half(e):
+        return wdn_all.at[
+            pl.ds(pl.multiple_of(wrap(z + NZ - e, NZ) * 384 + c * 192, 192), 192), :]
+
+    def dn_piece(e):
+        return down_rows(wrap(z + NZ - e, NZ))
+
+    gu_over_x = group(
+        [remote(gu_piece(e, w), gu_piece(e, w), *pair_of(9), dev) for e in others for dev in xdev],
+        9, wgu_all.at[0:432, 0:1152])
+    dn_over_y = group(
+        [remote(dn_piece(e), dn_piece(e), *pair_of(10), dev) for e in others for dev in ydev],
+        10, wdn_all.at[0:432, :])
+    o_over_y = [
+        [remote(o_piece(e), o_piece(e), s["ss"].at[11], s["os"].at[d - 1], ydev[d - 1]) for e in others]
+        for d in range(1, NY)]
+    o_sent = remote(wo_all.at[0:432, 0:384], wo_all.at[0:432, 0:384], s["ss"].at[11], s["os"].at[0], sib)
+    own_over_c = group(
+        [remote(gu_piece(e, w), gu_piece(e, w), *pair_of(12), sib) for e in others], 12, wgu_all.at[0:432, 0:384])
+    gu_over_c = group(
+        [remote(gu_piece(e, wrap(w + d, NX)), gu_piece(e, wrap(w + d, NX)), *pair_of(13), sib)
+         for e in others for d in range(1, NX)], 13, wgu_all.at[0:432, 0:1152])
+    dn_over_c = group(
+        [remote(dn_half(e), dn_half(e), *pair_of(14), sib) for e in others], 14, wdn_all.at[0:576, :])
+    o_over_c = []
+    for core, cols in enumerate((slice(0, 512), slice(512, 640))):
+        o_over_c.append(
+            group(
+                [remote(wo_all.at[block_rows(e, 144), cols], wo_all.at[block_rows(e, 144), cols], *pair_of(15), sib)
+                 for e in others], 15, wo_all.at[0:432, cols]))
+
+    @pl.when(has_o)
+    def _():
+        for copies in o_over_y:
+            for copy in copies:
+                copy.start()
+
+    begin(dn_over_y)
+    begin(gu_over_x)
+    begin(own_over_c)
+
     @pl.when(always)
     def _():
         keep_a, keep_b = visible(512), visible(256)
@@ -651,60 +705,6 @@
             m_s[h] = peaks[h]
             l_s[h] = totals[h]
             ot_s[h] = outs[h]
-
-    gu_over_z[1].wait_recv()
-    dn_over_z[1].wait_recv()
-
-    @pl.when(has_o)
-    def _():
-        o_over_z[1].wait_recv()
-
-    def gu_piece(e, ww):
-        return wgu_all.at[block_rows(e, 144), pl.ds(pl.multiple_of((c * 4 + ww) * 384, 128), 384)]
-
-    def o_piece(e):
-        return wo_all.at[block_rows(e, 144), pl.ds(oc, 128)]
-
-    def dn_half(e):
-        return wdn_all.at[
-            pl.ds(pl.multiple_of(wrap(z + NZ - e, NZ) * 384 + c * 192, 192), 192), :]
-
-    def dn_piece(e):
-        return down_rows(wrap(z + NZ - e, NZ))
-
-    gu_over_x = group(
-        [remote(gu_piece(e, w), gu_piece(e, w), *pair_of(9), dev) for e in others for dev in xdev],
-        9, wgu_all.at[0:432, 0:1152])
-    dn_over_y = group(
-        [remote(dn_piece(e), dn_piece(e), *pair_of(10), dev) for e in others for dev in ydev],
-        10, wdn_all.at[0:432, :])
-    o_over_y = [
-        [remote(o_piece(e), o_piece(e), s["ss"].at[11], s["os"].at[d - 1], ydev[d - 1]) for e in others]
-        for d in range(1, NY)]
-    o_sent = remote(wo_all.at[0:432, 0:384], wo_all.at[0:432, 0:384], s["ss"].at[11], s["os"].at[0], sib)
-    own_over_c = group(
-        [remote(gu_piece(e, w), gu_piece(e, w), *pair_of(12), sib) for e in others], 12, wgu_all.at[0:432, 0:384])
-    gu_over_c = group(
-        [remote(gu_piece(e, wrap(w + d, NX)), gu_piece(e, wrap(w + d, NX)), *pair_of(13), sib)
-         for e in others for d in range(1, NX)], 13, wgu_all.at[0:432, 0:1152])
-    dn_over_c = group(
-        [remote(dn_half(e), dn_half(e), *pair_of(14), sib) for e in others], 14, wdn_all.at[0:576, :])
-    o_over_c = []
-    for core, cols in enumerate((slice(0, 512), slice(512, 640))):
-        o_over_c.append(
-            group(
-                [remote(wo_all.at[block_rows(e, 144), cols], wo_all.at[block_rows(e, 144), cols], *pair_of(15), sib)
-                 for e in others], 15, wo_all.at[0:432, cols]))
-
-    @pl.when(has_o)
-    def _():
-        for copies in o_over_y:
-            for copy in copies:
-                copy.start()
-
-    begin(dn_over_y)
-    begin(gu_over_x)
-    begin(own_over_c)
 
     def earlier(d, carry):
         @pl.when(d == NZ - 1)
@@ -1095,7 +1095,6 @@
         vecs.rc[0, 5 + t : 6 + t, :] = gain_row[:, 128 * t : 128 * t + 128]
     vecs.rc[0, 18:24, :] = jnp.zeros((6, 128), F32)
     vecs.start()
-    vecs.next(0)
     @pl.when(early)
     def _():
         red_q.first_sum()
@@ -1109,18 +1108,19 @@
         for i in range(3):
             new_states[i][k][...] = new[i]
 
+    vecs.next(0)
     red_gu.gather_forward()
-    @pl.when(late)
-    def _():
-        red_q.first_sum()
-        red_q.z_start()
-
-    vecs.next(1)
     red_dn.z_sum()
     red_dn.exchange_start()
     red_o.z_sum()
     red_o.exchange_start()
 
+    @pl.when(late)
+    def _():
+        red_q.first_sum()
+        red_q.z_start()
+
+    vecs.next(1)
     @pl.when(early)
     def _():
         red_q.z_sum()

time: 123 us -> 122 us (level)
  no operation moved by 1% of the time
where the time goes in v1:
time: 122 us
  Pallas kernels  121 us (99%)
    pallas_call x1, Pallas kernels, train(): pl.pallas_call(step_kernel, out_shape=(fast((D, ROWS)), fast((D, ROWS)),...  116 us
    pallas_call x1, Pallas kernels, store(): pl.pallas_call(store_kernel, out_shape=shapes, in_specs=[jax.tree.map(lam...  4.94 us

profile of v1, /device:TPU:1, one launch (start us, length us, event | category | flops | bytes accessed | tf_op | source)
XLA Modules:
  0.0 122.0 jit_solution(4686300868696810626)
XLA Ops:
  0.7 116.2 %train_step.1 = (f32[576,512]{1,0:T(8,128)S(1)}, f32[576,512]{1,0:T(8,128)S(1)}, f32[144,960]{1,0:T(8,128)S(1)}, f32[144,576]{1,0:T(8,128)S(1)}, f32[144,3072]{1...) custom-call(bf16[576,512]{1,0:T(8,128)(2,1)} %bitcast.13, ...), custom_call_target="tpu_custom_call" | custom-call | tf_op jit(solution)/shard_map/train_step/pallas_call | solution.py:1253
  116.8 4.9 %store.1 = (f32[576,512]{1,0:T(8,128)}, f32[576,512]{1,0:T(8,128)}, f32[144,960]{1,0:T(8,128)}, f32[144,576]{1,0:T(8,128)}, f32[144,3072]{1,0:T(8,128)}, /*index...) custom-call(f32[576,512]{1,0:T(8,128)S(1)} %get-tuple-element.51.sou, ...), custom_call_target="tpu_custom_call" | custom-call | tf_op jit(solution)/shard_map/store/pallas_call | solution.py:1298

commit v2 on v1

--- a/solution.py
+++ b/solution.py
@@ -707,7 +707,7 @@
             ot_s[h] = outs[h]
 
     def earlier(d, carry):
-        @pl.when(d == NZ - 1)
+        @pl.when(d == jnp.where(z == NZ - 2, NZ - 2, NZ - 1))
         def _():
             for dd in range(1, NY):
                 from_y = wrap(y + NY - dd, NY)

time: 122 us -> 122 us (level)
  no operation moved by 1% of the time
where the time goes in v2:
time: 122 us
  Pallas kernels  121 us (99%)
    pallas_call x1, Pallas kernels, train(): pl.pallas_call(step_kernel, out_shape=(fast((D, ROWS)), fast((D, ROWS)),...  116 us
    pallas_call x1, Pallas kernels, store(): pl.pallas_call(store_kernel, out_shape=shapes, in_specs=[jax.tree.map(lam...  4.94 us

profile of v2, /device:TPU:1, one launch (start us, length us, event | category | flops | bytes accessed | tf_op | source)
XLA Modules:
  0.0 121.7 jit_solution(13326756189919647065)
XLA Ops:
  0.7 115.9 %train_step.1 = (f32[576,512]{1,0:T(8,128)S(1)}, f32[576,512]{1,0:T(8,128)S(1)}, f32[144,960]{1,0:T(8,128)S(1)}, f32[144,576]{1,0:T(8,128)S(1)}, f32[144,3072]{1...) custom-call(bf16[576,512]{1,0:T(8,128)(2,1)} %bitcast.13, ...), custom_call_target="tpu_custom_call" | custom-call | tf_op jit(solution)/shard_map/train_step/pallas_call | solution.py:1253
  116.6 4.9 %store.1 = (f32[576,512]{1,0:T(8,128)}, f32[576,512]{1,0:T(8,128)}, f32[144,960]{1,0:T(8,128)}, f32[144,576]{1,0:T(8,128)}, f32[144,3072]{1,0:T(8,128)}, /*index...) custom-call(f32[576,512]{1,0:T(8,128)S(1)} %get-tuple-element.51.sou, ...), custom_call_target="tpu_custom_call" | custom-call | tf_op jit(solution)/shard_map/store/pallas_call | solution.py:1298
